TPU v7x, 512 devices: a whole 4x8x8 slice. The times are simulated.
512 devices in a mesh: freq: 16 (over z, y_hi), strip: 32 (over x, y_lo, core).
Axes of the slice: x: 4, y: 8 (y_hi: 2, y_lo: 4; y = y_hi * 4 + y_lo), z: 8, core: 2. Of those that a mesh axis runs over, the one named last changes fastest.
Arguments:
- receiver_field: float32 [2, 16, 256, 2048], P(None, 'freq', 'strip'), may hold values from -17 to 17
- source_field: float32 [2, 16, 256, 2048], P(None, 'freq', 'strip'), may hold values from -4 to 4
- velocity_class: int32 [256, 2048], P('strip'), may hold values from 0 to 7
- filters: float32 [16, 8, 2, 9], P('freq'), may hold values from -0.8 to 0.8
- point_spread: float32 [16, 2, 15, 15], replicated, may hold values from -0.05 to 1
- spread_index: int32 [32, 16], replicated, may hold values from 0 to 15
Outputs:
- migrated: float32 [256, 2, 2048], P('strip', None, 'freq')
- reflectivity: float32 [256, 2, 2048], P('strip', None, 'freq')
- misfit: float32 [], replicated
All inputs are finite; a program needn't handle non-finite values.
Results may differ from a plain program's by a relative error of at most 0.0003.
Values sent between devices are 32-bit elements; how exact they have to be, the bound alone decides.
No kernel may reach another device: no remote copies, remote signals or barrier semaphores. Data moves between devices by JAX's collectives and lax.ppermute only.
A program may use at most 64 MiB of HBM per device.

v0:
```python
import math
import jax
import jax.numpy as jnp
from jax import lax
from jax.sharding import PartitionSpec as P

STEPS = 2
NCLASS = 8
PASSES = 2
HIGHEST = lax.Precision.HIGHEST


def extended_2(cells, sides, width):
    for axis, dim in sides:
        count = lax.axis_size(axis)
        ends = count - 1
        head = lax.slice_in_dim(cells, 0, width, axis=dim)
        tail = lax.slice_in_dim(cells, cells.shape[dim] - width, cells.shape[dim], axis=dim)
        cells = jnp.concatenate(
            [
                lax.ppermute(tail, axis, [(i, (i + 1) % count) for i in range(ends)]),
                cells,
                lax.ppermute(head, axis, [((i + 1) % count, i) for i in range(ends)]),
            ],
            axis=dim,
        )
    return cells


def class_maps(classes, filters):
    levels = jnp.arange(NCLASS, dtype=jnp.int32)
    chosen = jnp.where(classes[None] == levels[:, None, None], 1.0, 0.0)
    planes = jnp.einsum("fcpt,cxy->ptfxy", filters, chosen, precision=HIGHEST)
    taps_real = [planes[0, tap_index] for tap_index in range(9)]
    taps_imag = [planes[1, tap_index] for tap_index in range(9)]
    return (taps_real, taps_imag)


def advance(wavefield, taps_real, taps_imag, factor):
    row_count = wavefield.shape[2] - 2
    col_count = wavefield.shape[3]
    padded = jnp.pad(wavefield, ((0, 0), (0, 0), (0, 0), (1, 1)))
    real_part = jnp.zeros(taps_real[0].shape, jnp.float32)
    imag_part = jnp.zeros(taps_real[0].shape, jnp.float32)
    for tap_index in range(9):
        row_shift = tap_index // 3
        col_shift = tap_index % 3
        near_real = padded[
            0, :, row_shift : row_shift + row_count, col_shift : col_shift + col_count
        ]
        near_imag = padded[
            1, :, row_shift : row_shift + row_count, col_shift : col_shift + col_count
        ]
        coef_real = taps_real[tap_index]
        coef_imag = factor * taps_imag[tap_index]
        real_part = real_part + coef_real * near_real - coef_imag * near_imag
        imag_part = imag_part + coef_real * near_imag + coef_imag * near_real
    return jnp.stack([real_part, imag_part])


def correlate(receiver, source):
    return jnp.sum(receiver[0] * source[0] + receiver[1] * source[1], axis=0)


def lag_pick(lag_count):
    depths = jnp.arange(lag_count, dtype=jnp.int32)
    spacing = jnp.abs(depths[:, None] - depths[None, :])
    return jnp.where(spacing[None] == depths[:, None, None], 1.0, 0.0)


def convolve(extended, toeplitz, out_rows, picker):
    shifted = jnp.stack(
        [extended[shift_row : shift_row + out_rows] for shift_row in range(toeplitz.shape[0])],
        axis=2,
    )
    mixed = jnp.einsum("xdas,asly->xdly", shifted, toeplitz, precision=HIGHEST)
    return jnp.einsum("xdly,lde->xey", mixed, picker, precision=HIGHEST)


def local(receiver_field, source_field, velocity_class, filters, point_spread, spread_index):
    per_device = receiver_field.shape[1]
    row_count = receiver_field.shape[2]
    strips = lax.axis_size("strip")
    groups = lax.axis_size("freq")
    scaling = 1.0 / math.sqrt(per_device * groups)
    image_terms = []
    taps_real, taps_imag = class_maps(velocity_class, filters)
    receiver = receiver_field
    source = source_field
    for depth_step in range(STEPS):
        wide_receiver, wide_source = (
            extended_2(receiver, (("strip", 2),), 1),
            extended_2(source, (("strip", 2),), 1),
        )
        receiver = advance(wide_receiver, taps_real, taps_imag, 1.0)
        source = advance(wide_source, taps_real, taps_imag, -1.0)
        image_terms.append(correlate(receiver, source))
    partial_value = jnp.stack(image_terms, axis=1)
    whole = lax.psum(partial_value, "freq")
    share = whole.shape[2] // groups
    migrated = lax.dynamic_slice_in_dim(whole, lax.axis_index("freq") * share, share, 2)
    migrated = migrated * scaling
    col_count = migrated.shape[2]
    kernel_side = point_spread.shape[2]
    reach = kernel_side // 2
    wide_cols = col_count + 2 * reach
    picker = lag_pick(point_spread.shape[1])
    brick_row = lax.axis_index("strip")
    brick_col = lax.axis_index("freq")

    def brick_kernel(row_step, col_step):
        row_at = jnp.clip(brick_row + row_step, 0, strips - 1)
        col_at = jnp.clip(brick_col + col_step, 0, groups - 1)
        chosen = lax.dynamic_index_in_dim(
            lax.dynamic_index_in_dim(spread_index, row_at, 0, False), col_at, 0, False
        )
        return lax.dynamic_index_in_dim(point_spread, chosen, 0, False)

    columns = jnp.arange(wide_cols, dtype=jnp.int32)[:, None]
    outputs = jnp.arange(col_count, dtype=jnp.int32)[None, :]
    offsets = jnp.arange(kernel_side, dtype=jnp.int32)[:, None, None]
    band_forward = jnp.where(columns[None] - outputs[None] == offsets, 1.0, 0.0)
    band_adjoint = jnp.where(outputs[None] + 2 * reach - columns[None] == offsets, 1.0, 0.0)
    table_forward = jnp.einsum("lab,bsy->asly", brick_kernel(0, 0), band_forward, precision=HIGHEST)
    region = jnp.where(columns[:, 0] < reach, 0, jnp.where(columns[:, 0] < reach + col_count, 1, 2))
    region_pick = jnp.where(region[:, None] == jnp.arange(3, dtype=jnp.int32)[None, :], 1.0, 0.0)

    def table_adjoint(row_step):
        flipped = jnp.stack(
            [jnp.flip(brick_kernel(row_step, col_step), axis=1) for col_step in (-1, 0, 1)]
        )
        per_column = jnp.einsum("sj,jlab->slab", region_pick, flipped, precision=HIGHEST)
        return jnp.einsum("slab,bsw->aslw", per_column, band_adjoint, precision=HIGHEST)

    table_upper = table_adjoint(-1)
    table_middle = table_adjoint(0)
    table_lower = table_adjoint(1)

    def extend_rim(values):
        return extended_2(values, (("freq", 2), ("strip", 0)), reach)

    def measure(residual):
        return lax.psum(jnp.sum(residual * residual), ("freq", "strip"))

    cell_count = float(migrated.shape[1] * row_count * strips * col_count * groups)
    residual = -migrated
    reflectivity = jnp.zeros_like(migrated)
    energy = measure(residual)
    for pass_index in range(PASSES):
        weight = 1.0 / jnp.sqrt(residual * residual + energy / cell_count)
        extended = extend_rim(weight * residual)
        positions = jnp.arange(row_count + 2 * reach, dtype=jnp.int32)[:, None, None]
        middle = extended * jnp.where(
            (positions >= reach) & (positions < reach + row_count), 1.0, 0.0
        )
        summed = convolve(middle, table_middle, row_count, picker)
        upper = extended[: 3 * reach] * jnp.where(positions[: 3 * reach] < reach, 1.0, 0.0)
        lower = extended[row_count - reach :] * jnp.where(
            positions[row_count - reach :] >= row_count + reach, 1.0, 0.0
        )
        summed = summed.at[:reach].add(convolve(upper, table_upper, reach, picker))
        summed = summed.at[row_count - reach :].add(convolve(lower, table_lower, reach, picker))
        image_of = convolve(extend_rim(summed), table_forward, row_count, picker)
        grad_square, curvature = lax.psum(
            (jnp.sum(summed * summed), jnp.sum(weight * image_of * image_of)), ("freq", "strip")
        )
        step_length = grad_square / curvature
        reflectivity = reflectivity - step_length * summed
        residual = residual - step_length * image_of
        energy = measure(residual)
    return (migrated, reflectivity, energy / cell_count)


def solution(mesh):
    return jax.shard_map(
        local,
        mesh=mesh,
        in_specs=(
            P(None, "freq", "strip", None),
            P(None, "freq", "strip", None),
            P("strip", None),
            P("freq", None, None, None),
            P(),
            P(),
        ),
        out_specs=(P("strip", None, "freq"), P("strip", None, "freq"), P()),
        check_vma=False,
    )
```

profile of v0, /device:TPU:1, one launch (start us, length us, event | category | flops | bytes accessed | tf_op | source)
XLA Modules:
  0.0 950.9 jit_solution(10511014915909429593)
XLA Ops:
  8.9 4.6 collective-permute-start.2
  13.5 6.1 collective-permute-start.3
  21.2 1.9 collective-permute-start
  23.1 3.0 collective-permute-start.1
  26.1 1.7 fusion.379
  45.8 3.2 constant_dynamic-slice_fusion.2
  50.7 2.6 copy.115
  57.8 3.9 copy.109
  61.7 3.7 convolution_bitcast_fusion.2
  65.4 3.7 convolution_bitcast_fusion.3
  71.2 1.9 convolution_bitcast_fusion
  73.1 3.9 copy.102
  79.6 1.8 fusion.80
  81.4 1.8 fusion.77
  85.8 1.6 fusion.75
  87.4 1.6 fusion.73
  89.1 4.1 fusion.282
  93.2 2.6 collective-permute-start.6
  95.8 1.9 collective-permute-start.7
  97.8 3.6 collective-permute-start.4
  101.4 1.9 collective-permute-start.5
  103.8 2.7 collective-permute-done.5
  106.9 4.6 fusion.281
  112.3 5.4 convolution_bitcast_fusion.4
  117.8 193.8 %all-reduce.8.cloned.1.call-done = f32[8,2,2048]{2,1,0:T(2,128)} async-done(((f32[8,2,2048]{2,1,0:T(2,128)}), f32[8,2,2048]{2,1,0:T(2,128)}) %all-reduce.8.cloned.1.call-update) | async-done | bytes 131088 | tf_op jit(solution)/shard_map/psum | solution.py:99
  311.6 1.3 multiply_reduce_fusion.4
  312.9 106.4 %psum.57 = f32[]{:T(128)} all-reduce(f32[]{:T(128)} %get-tuple-element.61), channel_id=1, replica_groups=mesh['freq'=16,'strip'=32] {'freq','strip'}, use_global_device_ids=true, to_apply=%region_2.3 | all-reduce | flops 1 | bytes 8 | tf_op jit(solution)/shard_map/psum | solution.py:143
  420.0 5.6 collective-permute-start.8
  425.6 1.3 collective-permute-start.9
  427.0 7.0 collective-permute-done.9
  434.0 2.6 collective-permute-start.10
  436.7 2.8 collective-permute-start.11
  439.6 2.2 collective-permute-done.11
  442.5 4.2 fusion.14
  447.1 2.5 fusion.6
  449.5 2.5 fusion.10
  452.8 6.0 collective-permute-start.12
  458.7 1.3 collective-permute-start.13
  460.0 2.0 convolution_bitcast_fusion.1
  462.1 5.0 collective-permute-done.13
  467.2 3.4 collective-permute-start.14
  470.5 2.1 collective-permute-start.15
  473.3 2.3 collective-permute-done.15
  476.0 2.4 fusion.2
  479.3 103.4 %all-reduce.5 = (f32[]{:T(128)}, f32[]{:T(128)}) all-reduce(f32[]{:T(128)} %multiply_reduce_fusion.2, f32[]{:T(128)} %get-tuple-element.117), channel_id=1, replica_groups=mesh['freq'=16,'strip'=32] {'freq','strip'}, use_global_device_ids=true, to_apply=%region_4.5 | all-reduce | flops 2 | bytes 16 | tf_op jit(solution)/shard_map/psum | solution.py:164
  584.6 95.3 %psum.60 = f32[]{:T(128)} all-reduce(f32[]{:T(128)} %get-tuple-element.57), channel_id=1, replica_groups=mesh['freq'=16,'strip'=32] {'freq','strip'}, use_global_device_ids=true, to_apply=%region_8.9 | all-reduce | flops 1 | bytes 8 | tf_op jit(solution)/shard_map/psum | solution.py:143
  680.6 4.8 collective-permute-start.16
  685.4 1.3 collective-permute-start.17
  686.8 7.0 collective-permute-done.17
  693.9 2.6 collective-permute-start.18
  696.5 2.7 collective-permute-start.19
  699.2 2.3 collective-permute-done.19
  701.9 4.1 fusion.4
  706.3 2.5 fusion.8
  709.0 2.4 fusion.12
  712.4 6.5 collective-permute-start.20
  719.0 1.3 collective-permute-start.21
  720.3 7.0 collective-permute-done.21
  727.4 3.4 collective-permute-start.22
  730.8 1.9 collective-permute-start.23
  733.3 2.5 collective-permute-done.23
  736.2 2.4 fusion
  739.5 104.5 %all-reduce.4 = (f32[]{:T(128)}, f32[]{:T(128)}) all-reduce(f32[]{:T(128)} %multiply_reduce_fusion.1, f32[]{:T(128)} %get-tuple-element.119), channel_id=1, replica_groups=mesh['freq'=16,'strip'=32] {'freq','strip'}, use_global_device_ids=true, to_apply=%region_10.11 | all-reduce | flops 2 | bytes 16 | tf_op jit(solution)/shard_map/psum | solution.py:164
  846.6 95.3 %psum.63 = f32[]{:T(128)} all-reduce(f32[]{:T(128)} %multiply_reduce_fusion), channel_id=1, replica_groups=mesh['freq'=16,'strip'=32] {'freq','strip'}, use_global_device_ids=true, to_apply=%region_14.15 | all-reduce | flops 1 | bytes 8 | tf_op jit(solution)/shard_map/psum | solution.py:143
  (250 shorter events, 28.8 us)
Async XLA Ops:
  7.2 38.7 %copy-start.4 = (f32[16,2,15,15]{0,1,3,2:T(2,128)S(1)}, f32[16,2,15,15]{0,1,3,2:T(2,128)}, u32[]{:S(2)}) copy-start(f32[16,2,15,15]{0,1,3,2:T(2,128)} %param.18) | copy-start | bytes 86404
  7.2 304.4 %all-reduce.8.cloned.1.call-start = ((), (), s32[]{:S(2)}) async-start(), calls=%async_computation | async-start | bytes 262144 | tf_op jit(solution)/shard_map/psum | solution.py:99
  8.9 68.2 %collective-permute-start.2 = (f32[2,1,1,2048]{3,0,2,1:T(2,128)}, f32[2,1,1,2048]{3,0,2,1:T(2,128)}, u32[]{:S(2)}, u32[]{:S(2)}) collective-permute-start(f32[2,1,1,2048]{3,0,2,1:T(2,128)} %get-tuple-element.82), channel_id=1, source_target_pairs={{0,1},{1,2},{2,3},{3,4},{4,5},{5,6},{6,7},{7,8},{8,9},{9,10},{10,1... | collective-permute-start | bytes 49160 | tf_op jit(solution)/shard_map/ppermute | solution.py:21
  13.5 64.4 %collective-permute-start.3 = (f32[2,1,1,2048]{3,0,2,1:T(2,128)}, f32[2,1,1,2048]{3,0,2,1:T(2,128)}, u32[]{:S(2)}, u32[]{:S(2)}) collective-permute-start(f32[2,1,1,2048]{3,0,2,1:T(2,128)} %get-tuple-element.83), channel_id=1, source_target_pairs={{1,0},{2,1},{3,2},{4,3},{5,4},{6,5},{7,6},{8,7},{9,8},{10,9},{11,1... | collective-permute-start | bytes 49160 | tf_op jit(solution)/shard_map/ppermute | solution.py:23
  21.2 62.0 %collective-permute-start = (f32[2,1,1,2048]{3,0,2,1:T(2,128)}, f32[2,1,1,2048]{3,0,2,1:T(2,128)}, u32[]{:S(2)}, u32[]{:S(2)}) collective-permute-start(f32[2,1,1,2048]{3,0,2,1:T(2,128)} %get-tuple-element.78), channel_id=1, source_target_pairs={{0,1},{1,2},{2,3},{3,4},{4,5},{5,6},{6,7},{7,8},{8,9},{9,10},{10,1... | collective-permute-start | bytes 49160 | tf_op jit(solution)/shard_map/ppermute | solution.py:21
  23.1 61.0 %collective-permute-start.1 = (f32[2,1,1,2048]{3,0,2,1:T(2,128)}, f32[2,1,1,2048]{3,0,2,1:T(2,128)}, u32[]{:S(2)}, u32[]{:S(2)}) collective-permute-start(f32[2,1,1,2048]{3,0,2,1:T(2,128)} %get-tuple-element.79), channel_id=1, source_target_pairs={{1,0},{2,1},{3,2},{4,3},{5,4},{6,5},{7,6},{8,7},{9,8},{10,9},{11,1... | collective-permute-start | bytes 49160 | tf_op jit(solution)/shard_map/ppermute | solution.py:23
  49.1 4.3 copy-start.14
  61.7 3.7 copy-start.5
  65.4 3.8 copy-start.7
  65.4 4.1 copy-start.6
  65.4 5.8 copy-start.11
  65.4 5.8 copy-start.12
  71.2 6.6 copy-start.8
  79.6 4.3 copy-start.9
  93.2 10.1 %collective-permute-start.6 = (f32[2,1,1,2048]{3,0,2,1:T(2,128)S(1)}, f32[2,1,1,2048]{3,0,2,1:T(2,128)S(1)}, u32[]{:S(2)}, u32[]{:S(2)}) collective-permute-start(f32[2,1,1,2048]{3,0,2,1:T(2,128)S(1)} %get-tuple-element.73), channel_id=1, source_target_pairs={{0,1},{1,2},{2,3},{3,4},{4,5},{5,6},{6,7},{7,8},{8,9},{9,10},{10,1... | collective-permute-start | bytes 49160 | tf_op jit(solution)/shard_map/ppermute | solution.py:21
  95.8 7.6 collective-permute-start.7
  97.8 6.0 collective-permute-start.4
  101.4 5.1 collective-permute-start.5
  112.3 329.5 %copy-start.13 = (f32[21]{0:T(128)S(1)}, f32[21]{0:T(128)}, u32[]{:S(2)}) copy-start(f32[21]{0:T(128)} %fusion.337) | copy-start | bytes 256
  117.8 329.3 %copy-start.2 = (f32[15,142,2,128,1]{3,0,2,1,4:T(8,128)S(1)}, f32[15,142,2,128,1]{3,0,2,1,4:T(8,128)}, u32[]{:S(2)}) copy-start(f32[15,142,2,128,1]{3,0,2,1,4:T(8,128)} %convolution_bitcast_fusion.2) | copy-start | bytes 6543364
  312.9 271.1 %copy-start.10 = (f32[8,2,128]{2,1,0:T(2,128)}, f32[8,2,128]{2,1,0:T(2,128)S(1)}, u32[]{:S(2)}) copy-start(f32[8,2,128]{2,1,0:T(2,128)S(1)} %get-tuple-element.62) | copy-start | bytes 24580
  420.0 7.0 collective-permute-start.8
  425.6 8.3 collective-permute-start.9
  434.0 5.5 collective-permute-start.10
  436.7 5.0 collective-permute-start.11
  442.5 7.0 copy-start
  452.8 9.3 collective-permute-start.12
  458.7 8.3 collective-permute-start.13
  467.2 6.1 collective-permute-start.14
  470.5 5.0 collective-permute-start.15
  680.5 25.7 %copy-start.1 = (f32[15,142,2,128,1]{3,0,2,1,4:T(8,128)S(1)}, f32[15,142,2,128,1]{3,0,2,1,4:T(8,128)}, u32[]{:S(2)}) copy-start(f32[15,142,2,128,1]{3,0,2,1,4:T(8,128)} %convolution_bitcast_fusion.3) | copy-start | bytes 6543364
  680.6 6.1 collective-permute-start.16
  685.4 8.3 collective-permute-start.17
  693.9 5.3 collective-permute-start.18
  696.5 5.0 collective-permute-start.19
  706.1 2.9 copy-start.3
  712.4 7.8 collective-permute-start.20
  719.0 8.3 collective-permute-start.21
  727.4 5.9 collective-permute-start.22
  730.8 5.0 collective-permute-start.23
Sparse Core Ops, SparseCore 0:
  112.4 199.0 all-reduce.7
where the time goes:
time: 962 us; the launch traced here: 951 us
  blocking collectives  505 us (52%)
  waiting for transfers between devices  232 us (24%)
  starting transfers between devices  75.2 us (8%)
  matrix products  45.8 us (5%)
  between operations  38.4 us (4%)
  local copies, waits for them, and re-layouts  28.9 us (3%)
  other arithmetic  26 us (3%)
    psum x3, blocking collectives, measure(): return lax.psum(jnp.sum(residual * residual), ('freq', 'strip'))  297 us
    psum x2, blocking collectives, local(): lax.psum((jnp.sum(summed * summed), jnp.sum(weight * image_of * image_of)...  208 us
    psum x1, waiting for transfers between devices, local(): whole = lax.psum(partial_value, 'freq')  194 us
    ppermute x12, starting transfers between devices, extended_2(): lax.ppermute(tail, axis, [(i, (i + 1) % count) for i in range(ends)])  47.6 us
    ppermute x12, waiting for transfers between devices, extended_2(): lax.ppermute(head, axis, [((i + 1) % count, i) for i in range(ends)])  37.9 us
    ppermute x12, starting transfers between devices, extended_2(): lax.ppermute(head, axis, [((i + 1) % count, i) for i in range(ends)])  27.6 us
    dot_general x8, matrix products, convolve(): mixed = jnp.einsum('xdas,asly->xdly', shifted, toeplitz, precision=HIGHEST)  23 us
  transfers between devices with their start and end apart: 25, of which 10 were waited for; matrix products, arithmetic and copies ran while one was open for 5% of the time, Pallas kernels for 0%

commit v1 on v0

--- a/solution.py
+++ b/solution.py
@@ -96,7 +96,7 @@
         source = advance(wide_source, taps_real, taps_imag, -1.0)
         image_terms.append(correlate(receiver, source))
     partial_value = jnp.stack(image_terms, axis=1)
-    whole = lax.psum(partial_value, "freq")
+    whole = jnp.sum(lax.all_gather(partial_value, "freq"), axis=0)
     share = whole.shape[2] // groups
     migrated = lax.dynamic_slice_in_dim(whole, lax.axis_index("freq") * share, share, 2)
     migrated = migrated * scaling

time: 962 us -> 817 us (0.85)
  waiting for transfers between devices: 232 us -> 86.4 us
  matrix products: 45.8 us -> 56.4 us
    psum x1 -> x0, waiting for transfers between devices: 194 us -> none  [local(): whole = lax.psum(partial_value, 'freq')]
    all_gather x0 -> x1, waiting for transfers between devices: none -> 47.4 us  [local(): whole = jnp.sum(lax.all_gather(partial_value, 'freq'), axis=0)]
    dot_general x3, matrix products: 12.9 us -> 24.7 us  [table_adjoint(): jnp.einsum('slab,bsw->aslw', per_column, band_adjoint, precision=HIGHEST)]
  transfers between devices with their start and end apart: 25 -> 25, of which waited for: 10 -> 10; matrix products, arithmetic and copies ran while one was open for 5% -> 7% of each run, Pallas kernels for 0% -> 0%
where the time goes in v1:
time: 817 us; the launch traced here: 808 us
  blocking collectives  499 us (61%)
  waiting for transfers between devices  86.4 us (11%)
  starting transfers between devices  75.5 us (9%)
  matrix products  56.4 us (7%)
  between operations  39.5 us (5%)
  other arithmetic  25.9 us (3%)
  local copies, waits for them, and re-layouts  25.2 us (3%)
    psum x3, blocking collectives, measure(): return lax.psum(jnp.sum(residual * residual), ('freq', 'strip'))  293 us
    psum x2, blocking collectives, local(): lax.psum((jnp.sum(summed * summed), jnp.sum(weight * image_of * image_of)...  206 us
    ppermute x12, starting transfers between devices, extended_2(): lax.ppermute(tail, axis, [(i, (i + 1) % count) for i in range(ends)])  49.9 us
    all_gather x1, waiting for transfers between devices, local(): whole = jnp.sum(lax.all_gather(partial_value, 'freq'), axis=0)  47.4 us
    ppermute x12, waiting for transfers between devices, extended_2(): lax.ppermute(head, axis, [((i + 1) % count, i) for i in range(ends)])  39 us
    ppermute x12, starting transfers between devices, extended_2(): lax.ppermute(head, axis, [((i + 1) % count, i) for i in range(ends)])  25.6 us
    dot_general x3, matrix products, table_adjoint(): jnp.einsum('slab,bsw->aslw', per_column, band_adjoint, precision=HIGHEST)  24.7 us
    dot_general x8, matrix products, convolve(): mixed = jnp.einsum('xdas,asly->xdly', shifted, toeplitz, precision=HIGHEST)  22.6 us
  transfers between devices with their start and end apart: 25, of which 10 were waited for; matrix products, arithmetic and copies ran while one was open for 7% of the time, Pallas kernels for 0%

profile of v1, /device:TPU:1, one launch (start us, length us, event | category | flops | bytes accessed | tf_op | source)
XLA Modules:
  0.0 808.2 jit_solution(7308949430099930277)
XLA Ops:
  8.3 4.6 collective-permute-start.2
  12.9 5.5 collective-permute-start.3
  19.4 1.9 collective-permute-start
  21.3 2.4 collective-permute-start.1
  23.7 2.7 convolution_bitcast_fusion
  26.9 1.8 fusion.93
  28.7 1.8 fusion.90
  31.0 1.6 fusion.86
  32.6 1.6 fusion.88
  34.3 4.1 fusion.295
  38.4 3.2 collective-permute-start.6
  41.6 1.9 collective-permute-start.7
  43.6 3.6 collective-permute-start.4
  47.2 2.1 collective-permute-start.5
  49.7 2.7 collective-permute-done.5
  52.8 4.9 fusion.294
  76.7 3.0 constant_dynamic-slice_fusion.2
  81.4 2.9 copy.506
  85.5 1.2 copy.490
  88.7 3.9 copy.495
  94.2 3.9 copy.484
  98.3 3.7 convolution_bitcast_fusion.2
  102.0 18.6 %convolution_bitcast_fusion.3 = f32[15,142,2,128]{3,0,2,1:T(8,128)} fusion(f32[142,2,15,15]{3,2,1,0:T(8,128)S(1)} %copy-done.5, s32[142,128]{1,0:T(8,128)S(1)} %iota_subtract_fusion.1), kind=kOutput, calls=%fused_computation.27 | convolution fusion | flops 98695680 | bytes 2509424 | tf_op jit(solution)/shard_map/slab,bsw->aslw/dot_general | solution.py:133
  120.6 2.3 convolution_bitcast_fusion.4
  123.0 47.4 %all-gather.3.cloned.1.call-done = f32[128,2,2048]{2,1,0:T(2,128)} async-done(((f32[8,2,2048]{2,1,0:T(2,128)}), f32[128,2,2048]{2,1,0:T(2,128)}) %all-gather.3.cloned.1.call-update) | async-done | bytes 2097168 | tf_op jit(solution)/shard_map/all_gather | solution.py:99
  170.3 2.6 reduce_sum.80
  173.6 101.9 %psum.49 = f32[]{:T(128)} all-reduce(f32[]{:T(128)} %multiply_reduce_fusion.3), channel_id=1, replica_groups=mesh['freq'=16,'strip'=32] {'freq','strip'}, use_global_device_ids=true, to_apply=%region_2.3 | all-reduce | flops 1 | bytes 8 | tf_op jit(solution)/shard_map/psum | solution.py:143
  276.2 3.7 collective-permute-start.8
  280.0 1.3 collective-permute-start.9
  281.3 7.0 collective-permute-done.9
  288.4 4.6 collective-permute-start.10
  293.0 1.9 collective-permute-start.11
  295.0 3.1 collective-permute-done.11
  298.6 4.1 fusion.44
  303.0 2.4 fusion.38
  306.0 2.4 fusion.32
  309.1 6.2 collective-permute-start.12
  315.2 1.3 collective-permute-start.13
  316.5 2.0 convolution_bitcast_fusion.1
  318.6 5.0 collective-permute-done.13
  323.6 3.4 collective-permute-start.14
  327.0 1.9 collective-permute-start.15
  329.5 2.5 collective-permute-done.15
  332.4 2.4 fusion.50
  335.7 102.6 %all-reduce.5 = (f32[]{:T(128)}, f32[]{:T(128)}) all-reduce(f32[]{:T(128)} %multiply_reduce_fusion.1, f32[]{:T(128)} %fusion.323), channel_id=1, replica_groups=mesh['freq'=16,'strip'=32] {'freq','strip'}, use_global_device_ids=true, to_apply=%region_4.5 | all-reduce | flops 2 | bytes 16 | tf_op jit(solution)/shard_map/psum | solution.py:164
  440.3 95.6 %psum.52 = f32[]{:T(128)} all-reduce(f32[]{:T(128)} %get-tuple-element.69), channel_id=1, replica_groups=mesh['freq'=16,'strip'=32] {'freq','strip'}, use_global_device_ids=true, to_apply=%region_8.9 | all-reduce | flops 1 | bytes 8 | tf_op jit(solution)/shard_map/psum | solution.py:143
  536.6 6.7 collective-permute-start.16
  543.4 1.3 collective-permute-start.17
  544.7 7.0 collective-permute-done.17
  551.8 2.7 collective-permute-start.18
  554.4 2.8 collective-permute-start.19
  557.3 2.2 collective-permute-done.19
  559.9 4.1 fusion.47
  564.5 2.4 fusion.41
  567.4 2.4 fusion.35
  570.5 5.9 collective-permute-start.20
  576.4 1.3 collective-permute-start.21
  577.7 7.0 collective-permute-done.21
  584.8 3.4 collective-permute-start.22
  588.2 1.9 collective-permute-start.23
  590.7 2.5 collective-permute-done.23
  593.6 2.4 fusion.53
  597.5 103.8 %all-reduce.4 = (f32[]{:T(128)}, f32[]{:T(128)}) all-reduce(f32[]{:T(128)} %multiply_reduce_fusion, f32[]{:T(128)} %fusion.324), channel_id=1, replica_groups=mesh['freq'=16,'strip'=32] {'freq','strip'}, use_global_device_ids=true, to_apply=%region_10.11 | all-reduce | flops 2 | bytes 16 | tf_op jit(solution)/shard_map/psum | solution.py:164
  703.3 95.3 %psum.55 = f32[]{:T(128)} all-reduce(f32[]{:T(128)} %fusion.329), channel_id=1, replica_groups=mesh['freq'=16,'strip'=32] {'freq','strip'}, use_global_device_ids=true, to_apply=%region_14.15 | all-reduce | flops 1 | bytes 8 | tf_op jit(solution)/shard_map/psum | solution.py:143
  (262 shorter events, 22.1 us)
Async XLA Ops:
  7.2 19.3 %copy-start.7 = (f32[2,1,8,2048]{3,2,1,0:T(8,128)S(1)}, f32[2,1,8,2048]{3,2,1,0:T(8,128)}, u32[]{:S(2)}) copy-start(f32[2,1,8,2048]{3,2,1,0:T(8,128)} %param.15) | copy-start | bytes 393220
  7.2 163.1 %all-gather.3.cloned.1.call-start = ((), (), s32[]{:S(2)}) async-start(), calls=%async_computation | async-start | bytes 2228224 | tf_op jit(solution)/shard_map/all_gather | solution.py:99
  8.3 18.2 %collective-permute-start.2 = (f32[2,1,1,2048]{3,0,2,1:T(2,128)S(1)}, f32[2,1,1,2048]{3,0,2,1:T(2,128)S(1)}, u32[]{:S(2)}, u32[]{:S(2)}) collective-permute-start(f32[2,1,1,2048]{3,0,2,1:T(2,128)S(1)} %get-tuple-element.92), channel_id=1, source_target_pairs={{0,1},{1,2},{2,3},{3,4},{4,5},{5,6},{6,7},{7,8},{8,9},{9,10},{10,1... | collective-permute-start | bytes 49160 | tf_op jit(solution)/shard_map/ppermute | solution.py:21
  12.9 13.8 %collective-permute-start.3 = (f32[2,1,1,2048]{3,0,2,1:T(2,128)S(1)}, f32[2,1,1,2048]{3,0,2,1:T(2,128)S(1)}, u32[]{:S(2)}, u32[]{:S(2)}) collective-permute-start(f32[2,1,1,2048]{3,0,2,1:T(2,128)S(1)} %get-tuple-element.93), channel_id=1, source_target_pairs={{1,0},{2,1},{3,2},{4,3},{5,4},{6,5},{7,6},{8,7},{9,8},{10,9},{11,1... | collective-permute-start | bytes 49160 | tf_op jit(solution)/shard_map/ppermute | solution.py:23
  19.4 11.1 %collective-permute-start = (f32[2,1,1,2048]{3,0,2,1:T(2,128)S(1)}, f32[2,1,1,2048]{3,0,2,1:T(2,128)S(1)}, u32[]{:S(2)}, u32[]{:S(2)}) collective-permute-start(f32[2,1,1,2048]{3,0,2,1:T(2,128)S(1)} %get-tuple-element.88), channel_id=1, source_target_pairs={{0,1},{1,2},{2,3},{3,4},{4,5},{5,6},{6,7},{7,8},{8,9},{9,10},{10,1... | collective-permute-start | bytes 49160 | tf_op jit(solution)/shard_map/ppermute | solution.py:21
  21.3 9.4 %collective-permute-start.1 = (f32[2,1,1,2048]{3,0,2,1:T(2,128)S(1)}, f32[2,1,1,2048]{3,0,2,1:T(2,128)S(1)}, u32[]{:S(2)}, u32[]{:S(2)}) collective-permute-start(f32[2,1,1,2048]{3,0,2,1:T(2,128)S(1)} %get-tuple-element.89), channel_id=1, source_target_pairs={{1,0},{2,1},{3,2},{4,3},{5,4},{6,5},{7,6},{8,7},{9,8},{10,9},{11,1... | collective-permute-start | bytes 49160 | tf_op jit(solution)/shard_map/ppermute | solution.py:23
  26.9 3.6 copy-start.8
  38.4 10.9 %collective-permute-start.6 = (f32[2,1,1,2048]{3,0,2,1:T(2,128)S(1)}, f32[2,1,1,2048]{3,0,2,1:T(2,128)S(1)}, u32[]{:S(2)}, u32[]{:S(2)}) collective-permute-start(f32[2,1,1,2048]{3,0,2,1:T(2,128)S(1)} %get-tuple-element.83), channel_id=1, source_target_pairs={{0,1},{1,2},{2,3},{3,4},{4,5},{5,6},{6,7},{7,8},{8,9},{9,10},{10,1... | collective-permute-start | bytes 49160 | tf_op jit(solution)/shard_map/ppermute | solution.py:21
  41.6 7.7 collective-permute-start.7
  43.6 15.0 %copy-start.9 = (s32[32,16]{0,1:T(8,128)S(1)}, s32[32,16]{0,1:T(8,128)}, u32[]{:S(2)}) copy-start(s32[32,16]{0,1:T(8,128)} %param.19) | copy-start | bytes 6148
  43.6 6.1 collective-permute-start.4
  47.2 29.5 %copy-start.4 = (f32[16,2,15,15]{0,1,3,2:T(2,128)S(1)}, f32[16,2,15,15]{0,1,3,2:T(2,128)}, u32[]{:S(2)}) copy-start(f32[16,2,15,15]{0,1,3,2:T(2,128)} %param.18) | copy-start | bytes 86404
  47.2 5.2 collective-permute-start.5
  98.3 3.7 copy-start.5
  102.0 18.6 %copy-start.6 = (f32[142,2,15,15]{3,2,1,0:T(8,128)S(1)}, f32[142,2,15,15]{3,2,1,0:T(8,128)}, u32[]{:S(2)}) copy-start(f32[142,2,15,15]{3,2,1,0:T(8,128)} %copy.484) | copy-start | bytes 766804
  122.9 183.0 %copy-start = (f32[15,142,2,128]{3,0,2,1:T(8,128)}, f32[15,142,2,128]{3,0,2,1:T(8,128)S(1)}, u32[]{:S(2)}) copy-start(f32[15,142,2,128]{3,0,2,1:T(8,128)S(1)} %convolution_bitcast_fusion.4) | copy-start | bytes 6543364
  276.1 26.9 %copy-start.2 = (f32[15,142,2,128]{3,0,2,1:T(8,128)S(1)}, f32[15,142,2,128]{3,0,2,1:T(8,128)}, u32[]{:S(2)}) copy-start(f32[15,142,2,128]{3,0,2,1:T(8,128)} %convolution_bitcast_fusion.3) | copy-start | bytes 6543364
  276.2 5.0 collective-permute-start.8
  280.0 8.3 %collective-permute-start.9 = (f32[8,2,7]{2,0,1:T(8,128)S(1)}, f32[8,2,7]{2,0,1:T(8,128)S(1)}, u32[]{:S(2)}, u32[]{:S(2)}) collective-permute-start(f32[8,2,7]{2,0,1:T(8,128)S(1)} %get-tuple-element.131), channel_id=1, source_target_pairs={{32,0},{64,32},{96,64},{128,96},{160,128},{192,160},{224,192},{256... | collective-permute-start | bytes 1352 | tf_op jit(solution)/shard_map/ppermute | solution.py:23
  288.4 6.6 collective-permute-start.10
  293.0 5.1 collective-permute-start.11
  309.1 9.5 %collective-permute-start.12 = (f32[8,2,7]{2,0,1:T(8,128)S(1)}, f32[8,2,7]{2,0,1:T(8,128)S(1)}, u32[]{:S(2)}, u32[]{:S(2)}) collective-permute-start(f32[8,2,7]{2,0,1:T(8,128)S(1)} %get-tuple-element.117), channel_id=1, source_target_pairs={{0,32},{32,64},{64,96},{96,128},{128,160},{160,192},{192,224},{224... | collective-permute-start | bytes 1352 | tf_op jit(solution)/shard_map/ppermute | solution.py:21
  315.2 8.3 %collective-permute-start.13 = (f32[8,2,7]{2,0,1:T(8,128)S(1)}, f32[8,2,7]{2,0,1:T(8,128)S(1)}, u32[]{:S(2)}, u32[]{:S(2)}) collective-permute-start(f32[8,2,7]{2,0,1:T(8,128)S(1)} %get-tuple-element.118), channel_id=1, source_target_pairs={{32,0},{64,32},{96,64},{128,96},{160,128},{192,160},{224,192},{256... | collective-permute-start | bytes 1352 | tf_op jit(solution)/shard_map/ppermute | solution.py:23
  323.6 5.9 collective-permute-start.14
  327.0 5.1 collective-permute-start.15
  536.5 27.9 %copy-start.3 = (f32[15,142,2,128]{3,0,2,1:T(8,128)S(1)}, f32[15,142,2,128]{3,0,2,1:T(8,128)}, u32[]{:S(2)}) copy-start(f32[15,142,2,128]{3,0,2,1:T(8,128)} %convolution_bitcast_fusion.3) | copy-start | bytes 6543364
  536.6 8.0 collective-permute-start.16
  543.4 8.3 %collective-permute-start.17 = (f32[8,2,7]{2,0,1:T(8,128)S(1)}, f32[8,2,7]{2,0,1:T(8,128)S(1)}, u32[]{:S(2)}, u32[]{:S(2)}) collective-permute-start(f32[8,2,7]{2,0,1:T(8,128)S(1)} %get-tuple-element.115), channel_id=1, source_target_pairs={{32,0},{64,32},{96,64},{128,96},{160,128},{192,160},{224,192},{256... | collective-permute-start | bytes 1352 | tf_op jit(solution)/shard_map/ppermute | solution.py:23
  551.8 5.5 collective-permute-start.18
  554.4 5.1 collective-permute-start.19
  563.9 3.5 copy-start.1
  570.5 7.2 collective-permute-start.20
  576.4 8.3 %collective-permute-start.21 = (f32[8,2,7]{2,0,1:T(8,128)S(1)}, f32[8,2,7]{2,0,1:T(8,128)S(1)}, u32[]{:S(2)}, u32[]{:S(2)}) collective-permute-start(f32[8,2,7]{2,0,1:T(8,128)S(1)} %get-tuple-element.111), channel_id=1, source_target_pairs={{32,0},{64,32},{96,64},{128,96},{160,128},{192,160},{224,192},{256... | collective-permute-start | bytes 1352 | tf_op jit(solution)/shard_map/ppermute | solution.py:23
  584.8 5.9 collective-permute-start.22
  588.2 5.1 collective-permute-start.23
Sparse Core Ops, SparseCore 0:
  58.6 111.6 all-gather.2
